TPU v7x, 256 devices: a whole 4x4x8 slice. The times are simulated.
256 devices in a mesh: leaf: 64 (over y, z, core), rhs: 4 (over x).
Axes of the slice: x: 4, y: 4, z: 8, core: 2. Of those that a mesh axis runs over, the one named last changes fastest.
Arguments:
- leaf_right: float32 [2048, 256, 128], P('leaf', 'rhs'), may hold values from -6 to 6
- upper_right: float32 [128, 256, 128], P('leaf', 'rhs'), may hold values from -6 to 6
- leaf_inverse: bfloat16 [2048, 128, 128], P(('leaf', 'rhs')), as said below
- upper_inverse: bfloat16 [128, 128, 128], P('leaf'), as said below
- update_blocks: bfloat16 [16384, 128, 128], P('leaf'), may hold values from -0.046875 to 0.046875
- block_target: int32 [16384, 1], P('leaf'), may hold values from 0 to 127; in each aligned block of 256 rows (0 to 255, 256 to 511, ...) at most 4 rows name the same one
- upper_place: int32 [128], replicated, may hold values from 0 to 127, each once
Outputs:
- leaf_solution: float32 [2048, 256, 128], P('leaf', 'rhs')
- upper_solution: float32 [128, 256, 128], P('leaf', 'rhs')
Inputs may be any that keep to these rules, and one draw needn't show every extreme that they name: `leaf_inverse`: lower triangular blocks, diagonal entries between 0.6 and 1.4. `upper_inverse`: lower triangular blocks, diagonal entries between 0.6 and 1.4. `block_target`: among the 256 blocks of one device no upper supernode is named more than 4 times, a bound that some block reaches. `upper_place`: each row of the upper arrays holds exactly one upper supernode.
All inputs are finite; a program needn't handle non-finite values.
Results may differ from a plain program's by a relative error of at most 0.0049.
Values may be sent and summed in bfloat16 or wider, within the bound.
A program may use at most 64 MiB of HBM per device.

v0:
```python
import jax
import jax.numpy as jnp
from jax import lax
from jax.sharding import PartitionSpec as P


def on_device(
    leaf_right, upper_right, leaf_inverse, upper_inverse, update_blocks, block_target, upper_place
):
    inverse_mine = lax.all_gather(leaf_inverse, "rhs", axis=0, tiled=True)
    leaf_rounded = leaf_right.astype(jnp.bfloat16)
    leaf_forward = jnp.einsum(
        "ncw,nvw->ncv", leaf_rounded, inverse_mine, preferred_element_type=jnp.float32
    )
    leaf_half = leaf_forward.astype(jnp.bfloat16)
    leaf_count, columns, width = leaf_forward.shape
    block_count = update_blocks.shape[0]
    per_leaf = block_count // leaf_count
    grouped = update_blocks.reshape(leaf_count, per_leaf, width, width)
    updates = jnp.einsum("ncw,nbvw->nbcv", leaf_half, grouped, preferred_element_type=jnp.float32)
    updates = updates.reshape(block_count, columns, width)
    upper_total = upper_place.shape[0]
    table = jnp.arange(upper_total, dtype=jnp.int32)
    position = jnp.sum(jnp.where(block_target == table[None, :], upper_place[None, :], 0), axis=1)
    upper_rows = upper_right.shape[0]
    local_index = position
    inside = (local_index >= 0) & (local_index < upper_rows * lax.axis_size("leaf"))
    local_index = jnp.where(inside, local_index, upper_rows * lax.axis_size("leaf"))
    upper_sums = lax.psum_scatter(
        jax.ops.segment_sum(updates, local_index, num_segments=upper_rows * lax.axis_size("leaf")),
        "leaf",
        scatter_dimension=0,
        tiled=True,
    )
    upper_rounded = (upper_right - upper_sums).astype(jnp.bfloat16)
    upper_half = jnp.einsum(
        "pcw,pvw->pcv", upper_rounded, upper_inverse, preferred_element_type=jnp.float32
    ).astype(jnp.bfloat16)
    upper_solution = jnp.einsum(
        "pcw,pwv->pcv", upper_half, upper_inverse, preferred_element_type=jnp.float32
    )
    upper_sent = upper_solution.astype(jnp.bfloat16)
    solved_table = lax.all_gather(upper_sent, "leaf", axis=0, tiled=True)
    chosen = jnp.take(solved_table, position, axis=0)
    corrections = jnp.einsum(
        "kcv,kvw->kcw", chosen, update_blocks, preferred_element_type=jnp.float32
    )
    corrections = corrections.reshape(leaf_count, per_leaf, columns, width).sum(axis=1)
    leaf_back = (leaf_forward - corrections).astype(jnp.bfloat16)
    leaf_solution = jnp.einsum(
        "ncw,nwv->ncv", leaf_back, inverse_mine, preferred_element_type=jnp.float32
    )
    return (leaf_solution, upper_solution)


def solution(mesh):
    return jax.shard_map(
        on_device,
        mesh=mesh,
        in_specs=(
            P("leaf", "rhs", None),
            P("leaf", "rhs", None),
            P(("leaf", "rhs"), None, None),
            P("leaf", None, None),
            P("leaf", None, None),
            P("leaf", None),
            P(),
        ),
        out_specs=(P("leaf", "rhs", None), P("leaf", "rhs", None)),
        check_vma=False,
    )
```

profile of v0, /device:TPU:1, one launch (start us, length us, event | category | flops | bytes accessed | tf_op | source)
XLA Modules:
  0.0 338.4 jit_solution(17346281940933567968)
XLA Ops:
  7.2 0.0 copy-start
  7.2 0.0 all-gather.3.cloned.1.call-start
  7.2 0.7 all-gather.3.cloned.1.call-update
  7.9 0.0 reduce-scatter.2.cloned.1.call-start
  8.0 0.9 select_reduce_fusion
  8.8 30.4 %all-gather.3.cloned.1.call-done = bf16[32,128,128]{2,1,0:T(8,128)(2,1)} async-done(((bf16[8,128,128]{2,1,0:T(8,128)(2,1)}), bf16[32,128,128]{2,1,0:T(8,128)(2,1)}) %all-gather.3.cloned.1.call-update) | async-done | bytes 1048592 | tf_op jit(solution)/shard_map/all_gather | solution.py:10
  39.2 2.3 fusion.11
  41.6 9.6 %fusion.8 = f32[32,64,8,128]{3,1,2,0:T(8,128)} fusion(bf16[32,8,128,128]{3,2,1,0:T(8,128)(2,1)} %bitcast.22, f32[32,64,128]{2,1,0:T(8,128)S(1)} %fusion.11), kind=kOutput, calls=%fused_computation.11 | convolution fusion | flops 537133056 | bytes 17825792 | tf_op jit(solution)/shard_map/ncw,nbvw->nbcv/dot_general | solution.py:20
  51.2 2.5 broadcast_in_dim.33
  53.7 39.9 %scatter_fusion = f32[128,64,128]{2,1,0:T(8,128)} fusion(f32[128,64,128]{2,1,0:T(8,128)} %broadcast_in_dim.33, s32[256]{0:T(256)S(1)} %bitcast.23, f32[256,64,128]{2,1,0:T(8,128)} %bitcast.21), kind=kCustom, calls=%fused_computation.1 | custom fusion | flops 2097152 | bytes 25166848 | tf_op jit(solution)/shard_map/scatter-add | solution.py:30
  93.6 0.0 copy-start.2
  93.6 0.0 reduce-scatter.2.cloned.1.call-update
  93.6 0.0 all-gather.5.cloned.1.call-start
  93.7 140.1 %reduce-scatter.2.cloned.1.call-done = f32[2,64,128]{2,1,0:T(8,128)} async-done(((f32[128,64,128]{2,1,0:T(8,128)}), f32[2,64,128]{2,1,0:T(8,128)}) %reduce-scatter.2.cloned.1.call-update) | async-done | bytes 65552 | tf_op jit(solution)/shard_map/reduce_scatter | solution.py:29
  233.8 0.0 copy-done
  233.8 0.0 copy-done.2
  233.8 1.7 fusion.14
  235.5 0.0 all-gather.5.cloned.1.call-update
  235.6 83.0 %all-gather.5.cloned.1.call-done = bf16[128,64,128]{2,1,0:T(8,128)(2,1)} async-done(((bf16[2,64,128]{2,1,0:T(8,128)(2,1)}), bf16[128,64,128]{2,1,0:T(8,128)(2,1)}) %all-gather.5.cloned.1.call-update) | async-done | bytes 2097168 | tf_op jit(solution)/shard_map/all_gather | solution.py:43
  318.6 4.6 %gather_fusion = bf16[256,64,128]{2,1,0:T(8,128)(2,1)} fusion(bf16[128,64,128]{2,1,0:T(8,128)(2,1)} %all-gather.5.cloned.1.call-done, s32[1024]{0:T(1024)S(1)} %pad_clamp_fusion), kind=kCustom, calls=%fused_computation | custom fusion | bytes 8389632 | tf_op jit(solution)/shard_map/jit(_take)/gather | solution.py:44
  323.3 0.0 copy-start.1
  323.3 7.2 %bitcast_reduce_fusion = f32[32,64,128]{2,1,0:T(8,128)S(1)} fusion(bf16[256,128,128]{2,1,0:T(8,128)(2,1)} %param.11, bf16[256,64,128]{2,1,0:T(8,128)(2,1)} %gather_fusion, pred[256]{0:T(512)(128)(4,1)S(1)} %compare_and_fusion), kind=kOutput, calls=%fused_computation.2 | convolution fusion | flops 540803072 | bytes 13631744 | tf_op jit(solution)/shard_map/kcv,kvw->kcw/dot_general | solution.py:45
  330.4 0.0 copy-done.1
  330.4 1.4 fusion.7
  (3 shorter events, 0.0 us)
Async XLA Ops:
  7.2 226.6 %copy-start = (bf16[2,128,128]{2,1,0:T(8,128)(2,1)S(1)}, bf16[2,128,128]{2,1,0:T(8,128)(2,1)}, u32[]{:S(2)}) copy-start(bf16[2,128,128]{2,1,0:T(8,128)(2,1)} %param.10) | copy-start | bytes 196612
  7.2 32.1 %all-gather.3.cloned.1.call-start = ((), (), s32[]{:S(2)}) async-start(), calls=%async_computation.1 | async-start | bytes 1310720 | tf_op jit(solution)/shard_map/all_gather | solution.py:10
  7.9 225.9 %reduce-scatter.2.cloned.1.call-start = ((), (), s32[]{:S(2)}) async-start(), calls=%async_computation.2 | async-start | bytes 4259840 | tf_op jit(solution)/shard_map/reduce_scatter | solution.py:29
  93.6 140.2 %copy-start.2 = (f32[2,64,128]{2,1,0:T(8,128)S(1)}, f32[2,64,128]{2,1,0:T(8,128)}, u32[]{:S(2)}) copy-start(f32[2,64,128]{2,1,0:T(8,128)} %param.8) | copy-start | bytes 196612
  93.6 225.0 %all-gather.5.cloned.1.call-start = ((), (), s32[]{:S(2)}) async-start(), calls=%async_computation.3 | async-start | bytes 2129920 | tf_op jit(solution)/shard_map/all_gather | solution.py:43
  323.3 7.2 %copy-start.1 = (bf16[32,128,128]{2,1,0:T(8,128)(2,1)S(1)}, bf16[32,128,128]{2,1,0:T(8,128)(2,1)}, u32[]{:S(2)}) copy-start(bf16[32,128,128]{2,1,0:T(8,128)(2,1)} %all-gather.3.cloned.1.call-done) | copy-start | bytes 3145732
Sparse Core Ops, SparseCore 0:
  9.8 29.3 all-gather.2
  93.8 139.9 reduce-scatter.1
  237.5 81.0 all-gather.4
where the time goes:
time: 339 us; the launch traced here: 338 us
  waiting for transfers between devices  254 us (75%)
  other arithmetic  40.8 us (12%)
  matrix products  22.3 us (7%)
  between operations  13.8 us (4%)
  local copies, waits for them, and re-layouts  7.11 us (2%)
    reduce_scatter x1, waiting for transfers between devices, on_device(): lax.psum_scatter(jax.ops.segment_sum(updates, local_index, num_segments=u...  140 us
    all_gather x1, waiting for transfers between devices, on_device(): solved_table = lax.all_gather(upper_sent, 'leaf', axis=0, tiled=True)  83 us
    scatter-add x1, other arithmetic, on_device(): jax.ops.segment_sum(updates, local_index, num_segments=upper_rows * lax.a...  39.9 us
    all_gather x1, waiting for transfers between devices, on_device(): inverse_mine = lax.all_gather(leaf_inverse, 'rhs', axis=0, tiled=True)  30.4 us
    dot_general x1, matrix products, on_device(): jnp.einsum('ncw,nbvw->nbcv', leaf_half, grouped, preferred_element_type=j...  9.63 us
    dot_general x1, matrix products, on_device(): jnp.einsum('kcv,kvw->kcw', chosen, update_blocks, preferred_element_type=...  7.16 us
  transfers between devices with their start and end apart: 3, of which 3 were waited for; matrix products, arithmetic and copies ran while one was open for 0% of the time, Pallas kernels for 0%

commit v1 on v0

--- a/solution.py
+++ b/solution.py
@@ -4,10 +4,31 @@
 from jax.sharding import PartitionSpec as P
 
 
+def collect(array, axis, dim):
+    size, index, extent = (lax.axis_size(axis), lax.axis_index(axis), array.shape[dim])
+    right = [(i, (i + 1) % size) for i in range(size)]
+    backward = [(i, (i - 1) % size) for i in range(size)]
+    whole = jnp.zeros((*array.shape[:dim], size * extent, *array.shape[dim + 1 :]), array.dtype)
+    whole = lax.dynamic_update_slice_in_dim(whole, array, index * extent, axis=dim)
+    from_left = from_right = array
+    middle = size // 2
+    for lap in range(1, middle + 1):
+        from_left = lax.ppermute(from_left, axis, right)
+        whole = lax.dynamic_update_slice_in_dim(
+            whole, from_left, (index - lap) % size * extent, axis=dim
+        )
+        if lap < size - middle:
+            from_right = lax.ppermute(from_right, axis, backward)
+            whole = lax.dynamic_update_slice_in_dim(
+                whole, from_right, (index + lap) % size * extent, axis=dim
+            )
+    return whole
+
+
 def on_device(
     leaf_right, upper_right, leaf_inverse, upper_inverse, update_blocks, block_target, upper_place
 ):
-    inverse_mine = lax.all_gather(leaf_inverse, "rhs", axis=0, tiled=True)
+    inverse_mine = collect(leaf_inverse, "rhs", 0)
     leaf_rounded = leaf_right.astype(jnp.bfloat16)
     leaf_forward = jnp.einsum(
         "ncw,nvw->ncv", leaf_rounded, inverse_mine, preferred_element_type=jnp.float32

time: 339 us -> 325 us (0.959)
  waiting for transfers between devices: 254 us -> 234 us
  starting transfers between devices: 0.12 us -> 5.41 us
    all_gather x1 -> x0, waiting for transfers between devices: 30.4 us -> none  [on_device(): inverse_mine = lax.all_gather(leaf_inverse, 'rhs', axis=0, tiled=True)]
    ppermute x0 -> x3, waiting for transfers between devices: none -> 6.91 us  [the longest x2 6.91 us: collect(): from_left = lax.ppermute(from_left, axis, right)]
    ppermute x0 -> x3, starting transfers between devices: none -> 5.33 us  [the longest x2 3.97 us: collect(): from_left = lax.ppermute(from_left, axis, right)]
    reduce_scatter x1, waiting for transfers between devices: 140 us -> 144 us  [on_device(): lax.psum_scatter(jax.ops.segment_sum(updates, local_index, num_segments=u...]
  transfers between devices with their start and end apart: 3 -> 5, of which waited for: 3 -> 4; matrix products, arithmetic and copies ran while one was open for 0% -> 1% of each run, Pallas kernels for 0% -> 0%
where the time goes in v1:
time: 325 us; the launch traced here: 324 us
  waiting for transfers between devices  234 us (72%)
  other arithmetic  40.3 us (12%)
  matrix products  21.9 us (7%)
  between operations  14.2 us (4%)
  local copies, waits for them, and re-layouts  8.44 us (3%)
  starting transfers between devices  5.41 us (2%)
    reduce_scatter x1, waiting for transfers between devices, on_device(): lax.psum_scatter(jax.ops.segment_sum(updates, local_index, num_segments=u...  144 us
    all_gather x1, waiting for transfers between devices, on_device(): solved_table = lax.all_gather(upper_sent, 'leaf', axis=0, tiled=True)  83.1 us
    scatter-add x1, other arithmetic, on_device(): jax.ops.segment_sum(updates, local_index, num_segments=upper_rows * lax.a...  39.4 us
    dot_general x1, matrix products, on_device(): jnp.einsum('ncw,nbvw->nbcv', leaf_half, grouped, preferred_element_type=j...  9.64 us
    dot_general x1, matrix products, on_device(): jnp.einsum('kcv,kvw->kcw', chosen, update_blocks, preferred_element_type=...  7.1 us
    ppermute x2, waiting for transfers between devices, collect(): from_left = lax.ppermute(from_left, axis, right)  6.91 us
  transfers between devices with their start and end apart: 5, of which 4 were waited for; matrix products, arithmetic and copies ran while one was open for 1% of the time, Pallas kernels for 0%

profile of v1, /device:TPU:1, one launch (start us, length us, event | category | flops | bytes accessed | tf_op | source)
XLA Modules:
  0.0 324.1 jit_solution(6959597418613802002)
XLA Ops:
  7.2 0.0 copy-start
  7.2 0.0 reduce-scatter.2.cloned.1.call-start
  7.2 2.1 collective-permute-start
  9.3 1.4 collective-permute-start.1
  10.7 0.9 select_reduce_fusion
  11.6 3.0 collective-permute-done
  14.6 1.9 collective-permute-start.2
  16.4 0.2 broadcast_in_dim.33
  16.7 1.0 constant_dynamic-update-slice_fusion.3
  17.8 0.0 collective-permute-done.1
  17.8 3.9 %collective-permute-done.2 = bf16[8,128,128]{2,1,0:T(8,128)(2,1)S(1)} collective-permute-done((bf16[8,128,128]{2,1,0:T(8,128)(2,1)S(1)}, bf16[8,128,128]{2,1,0:T(8,128)(2,1)S(1)}, u32[]{:S(2)}, u32[]{:S(2)}) %collective-permute-start.2) | collective-permute-done | bytes 262176 | tf_op jit(solution)/shard_map/ppermute | solution.py:16
  21.8 2.0 convolution_bitcast_fusion
  23.8 9.6 %fusion.8 = f32[32,64,8,128]{3,1,2,0:T(8,128)} fusion(bf16[32,8,128,128]{3,2,1,0:T(8,128)(2,1)} %bitcast.24, f32[32,64,128]{2,1,0:T(8,128)S(1)} %convolution_bitcast_fusion), kind=kOutput, calls=%fused_computation.12 | convolution fusion | flops 537133056 | bytes 17825792 | tf_op jit(solution)/shard_map/ncw,nbvw->nbcv/dot_general | solution.py:41
  33.5 2.5 broadcast_in_dim.37
  35.9 39.4 %scatter_fusion = f32[128,64,128]{2,1,0:T(8,128)} fusion(f32[128,64,128]{2,1,0:T(8,128)} %broadcast_in_dim.37, s32[256]{0:T(256)S(1)} %bitcast.25, f32[256,64,128]{2,1,0:T(8,128)} %bitcast.23), kind=kCustom, calls=%fused_computation.1 | custom fusion | flops 2097152 | bytes 25166848 | tf_op jit(solution)/shard_map/scatter-add | solution.py:51
  75.4 0.0 reduce-scatter.2.cloned.1.call-update
  75.4 0.0 all-gather.2.cloned.1.call-start
  75.4 143.8 %reduce-scatter.2.cloned.1.call-done = f32[2,64,128]{2,1,0:T(8,128)} async-done(((f32[128,64,128]{2,1,0:T(8,128)}), f32[2,64,128]{2,1,0:T(8,128)}) %reduce-scatter.2.cloned.1.call-update) | async-done | bytes 65552 | tf_op jit(solution)/shard_map/reduce_scatter | solution.py:50
  219.2 1.7 fusion.13
  221.0 0.0 all-gather.2.cloned.1.call-update
  221.0 83.1 %all-gather.2.cloned.1.call-done = bf16[128,64,128]{2,1,0:T(8,128)(2,1)} async-done(((bf16[2,64,128]{2,1,0:T(8,128)(2,1)}), bf16[128,64,128]{2,1,0:T(8,128)(2,1)}) %all-gather.2.cloned.1.call-update) | async-done | bytes 2097168 | tf_op jit(solution)/shard_map/all_gather | solution.py:64
  304.1 4.6 %gather_fusion = bf16[256,64,128]{2,1,0:T(8,128)(2,1)} fusion(bf16[128,64,128]{2,1,0:T(8,128)(2,1)} %all-gather.2.cloned.1.call-done, s32[1024]{0:T(1024)S(1)} %pad_clamp_fusion), kind=kCustom, calls=%fused_computation | custom fusion | bytes 8389632 | tf_op jit(solution)/shard_map/jit(_take)/gather | solution.py:65
  308.7 7.1 %bitcast_reduce_fusion = f32[32,64,128]{2,1,0:T(8,128)S(1)} fusion(bf16[256,128,128]{2,1,0:T(8,128)(2,1)} %param.11, bf16[256,64,128]{2,1,0:T(8,128)(2,1)} %gather_fusion, pred[256]{0:T(512)(128)(4,1)S(1)} %compare_and_fusion), kind=kOutput, calls=%fused_computation.2 | convolution fusion | flops 540803072 | bytes 13631744 | tf_op jit(solution)/shard_map/kcv,kvw->kcw/dot_general | solution.py:66
  315.8 1.4 fusion.7
  (9 shorter events, 0.1 us)
Async XLA Ops:
  7.2 212.1 %copy-start = (bf16[2,128,128]{2,1,0:T(8,128)(2,1)S(1)}, bf16[2,128,128]{2,1,0:T(8,128)(2,1)}, u32[]{:S(2)}) copy-start(bf16[2,128,128]{2,1,0:T(8,128)(2,1)} %param.10) | copy-start | bytes 196612
  7.2 212.1 %reduce-scatter.2.cloned.1.call-start = ((), (), s32[]{:S(2)}) async-start(), calls=%async_computation.1 | async-start | bytes 4259840 | tf_op jit(solution)/shard_map/reduce_scatter | solution.py:50
  7.2 7.4 %collective-permute-start = (bf16[8,128,128]{2,1,0:T(8,128)(2,1)}, bf16[8,128,128]{2,1,0:T(8,128)(2,1)S(1)}, u32[]{:S(2)}, u32[]{:S(2)}) collective-permute-start(bf16[8,128,128]{2,1,0:T(8,128)(2,1)} %param.9), channel_id=1, source_target_pairs={{0,1},{1,2},{2,3},{3,0},{4,5},{5,6},{6,7},{7,4},{8,9},{9,10},{10,1... | collective-permute-start | bytes 786440 | tf_op jit(solution)/shard_map/ppermute | solution.py:16
  9.3 8.4 %collective-permute-start.1 = (bf16[8,128,128]{2,1,0:T(8,128)(2,1)}, bf16[8,128,128]{2,1,0:T(8,128)(2,1)S(1)}, u32[]{:S(2)}, u32[]{:S(2)}) collective-permute-start(bf16[8,128,128]{2,1,0:T(8,128)(2,1)} %param.9), channel_id=1, source_target_pairs={{0,3},{1,0},{2,1},{3,2},{4,7},{5,4},{6,5},{7,6},{8,11},{9,8},{10,9... | collective-permute-start | bytes 786440 | tf_op jit(solution)/shard_map/ppermute | solution.py:21
  14.6 7.2 %collective-permute-start.2 = (bf16[8,128,128]{2,1,0:T(8,128)(2,1)S(1)}, bf16[8,128,128]{2,1,0:T(8,128)(2,1)S(1)}, u32[]{:S(2)}, u32[]{:S(2)}) collective-permute-start(bf16[8,128,128]{2,1,0:T(8,128)(2,1)S(1)} %collective-permute-done), channel_id=1, source_target_pairs={{0,1},{1,2},{2,3},{3,0},{4,5},{5,6},{6,7},{7,4},{8,9},{9,10},{10,1... | collective-permute-start | bytes 786440 | tf_op jit(solution)/shard_map/ppermute | solution.py:16
  75.4 143.9 %copy-start.1 = (f32[2,64,128]{2,1,0:T(8,128)S(1)}, f32[2,64,128]{2,1,0:T(8,128)}, u32[]{:S(2)}) copy-start(f32[2,64,128]{2,1,0:T(8,128)} %param.8) | copy-start | bytes 196612
  75.4 228.7 %all-gather.2.cloned.1.call-start = ((), (), s32[]{:S(2)}) async-start(), calls=%async_computation.2 | async-start | bytes 2129920 | tf_op jit(solution)/shard_map/all_gather | solution.py:64
Sparse Core Ops, SparseCore 0:
  75.5 143.6 reduce-scatter.1
  223.0 81.0 all-gather.1
